TPU v7x, 512 devices: a whole 4x8x8 slice. The times are simulated.
512 devices in a mesh: blk: 128 (over z, y, core), feat: 4 (over x).
Axes of the slice: x: 4, y: 8, z: 8, core: 2. Of those that a mesh axis runs over, the one named last changes fastest.
Arguments:
- feat_a: bfloat16 [2048, 64, 256], P('blk', 'feat'), may hold values from -25 to 25
- tiles_a: bfloat16 [2048, 8, 64, 64], P('blk', None, None, 'feat'), may hold values from -0.25 to 0.25
- owner_a: int32 [2048, 8], replicated, may hold values from 0 to 127, all different within a row; in each aligned block of 16 rows (0 to 15, 16 to 31, ...) at most 2 rows name the same one
- local_a: int32 [2048, 8], replicated, may hold values from 0 to 15
- feat_b: bfloat16 [2048, 64, 256], P('blk', 'feat'), may hold values from -25 to 25
- tiles_b: bfloat16 [2048, 8, 64, 64], P('blk', None, None, 'feat'), may hold values from -0.25 to 0.25
- owner_b: int32 [2048, 8], replicated, may hold values from 0 to 127, all different within a row; in each aligned block of 16 rows (0 to 15, 16 to 31, ...) at most 2 rows name the same one
- local_b: int32 [2048, 8], replicated, may hold values from 0 to 15
- weight: bfloat16 [256, 256], replicated, may hold values from -0.375 to 0.375
- cand_owner: int32 [256, 96], replicated, may hold values from 0 to 127, all different within a row; in each aligned block of 2 rows (0 to 1, 2 to 3, ...) at most 2 rows name the same one
- cand_local: int32 [256, 96], replicated, may hold values from 0 to 15
- target: int32 [2048, 64], P('blk'), may hold values from 0 to 6143
Outputs:
- grad_a: float32 [2048, 64, 256], P('blk', 'feat')
- grad_b: float32 [2048, 64, 256], P('blk', 'feat')
Inputs may be any that keep to these rules, and one draw needn't show every extreme that they name: `owner_a`: each row names 8 different blk indices; among the 16 rows of one blk index no value is named by more than 2 rows, and in every draw some value is named by exactly 2 rows of some blk index. `owner_b`: each row names 8 different blk indices; among the 16 rows of one blk index no value is named by more than 2 rows, and in every draw some value is named by exactly 2 rows of some blk index. `cand_owner`: each row names 96 different blk indices; in the aligned blocks of 2 rows (the groups of one blk index) no value is named by more than 2 rows, and in every draw some value is named by exactly 2 rows of some block.
All inputs are finite; a program needn't handle non-finite values.
Results may differ from a plain program's by a relative error of at most 0.029.
The roundings to bfloat16 on the way count: a program that leaves them out, or rounds other values in their place, can miss the bound.
Values may be sent and summed in bfloat16 or wider, within the bound.
No kernel may reach another device: no remote copies, remote signals or barrier semaphores. Data moves between devices by JAX's collectives and lax.ppermute only.
A program may use at most 64 MiB of HBM per device.

v0:
```python
import jax
import jax.numpy as jnp
from jax import lax
from jax.sharding import PartitionSpec as P

GA = 8


score_scale = 0.25


def sending_plan(owner_rows, within_rows, source, capacity):
    present = owner_rows == source
    position = jnp.cumsum(present.astype(jnp.int32), axis=1) - 1
    matches = present[:, :, None] & (
        position[:, :, None] == jnp.arange(capacity, dtype=jnp.int32)[None, None, :]
    )
    chosen = jnp.sum(jnp.where(matches, within_rows[:, :, None], 0), axis=1)
    filled = jnp.any(matches, axis=1)
    return (chosen, filled)


def arrival_slots(own_owners, capacity):
    requests = own_owners.shape[0]
    same_owner = own_owners[:, None] == own_owners[None, :]
    before = jnp.arange(requests)[None, :] < jnp.arange(requests)[:, None]
    earlier = jnp.sum((same_owner & before).astype(jnp.int32), axis=1)
    return own_owners * capacity + earlier


def link_plan(owner_full, within_full, peer_count, capacity, source):
    owner_rows = owner_full.reshape(peer_count, -1)
    within_rows = within_full.reshape(peer_count, -1)
    chosen, filled = sending_plan(owner_rows, within_rows, source, capacity)
    own_owners = lax.dynamic_index_in_dim(owner_rows, source, 0, keepdims=False)
    return (chosen, filled, arrival_slots(own_owners, capacity))


def outgoing_blocks(local_rows, chosen, filled):
    picked = jnp.take(local_rows, chosen, axis=0)
    return jnp.where(filled[:, :, None, None], picked, jnp.zeros((), picked.dtype))


def aggregate(tile_set, arrived, slot_index):
    peer_count, capacity, quarter, features = arrived.shape
    stacked = arrived.reshape(peer_count * capacity, quarter, features)
    neighbours = jnp.take(stacked, slot_index, axis=0).reshape(
        tile_set.shape[0], tile_set.shape[1], quarter, features
    )
    return jnp.einsum("bkrc,bkcd->brd", tile_set, neighbours, preferred_element_type=jnp.float32)


def embedding(local_features, summed, weight):
    blocks, quarter, features = local_features.shape
    propagated = (
        (local_features.astype(jnp.float32) + summed)
        .astype(jnp.bfloat16)
        .reshape(blocks * quarter, features)
    )
    preact = jnp.dot(propagated, weight, preferred_element_type=jnp.float32)
    return jnp.maximum(preact, 0.0).astype(jnp.bfloat16).reshape(blocks, quarter, features)


def per_device(
    feat_a,
    tiles_a,
    owner_a,
    local_a,
    feat_b,
    tiles_b,
    owner_b,
    local_b,
    weight,
    cand_owner,
    cand_local,
    target,
):
    peer_count = lax.axis_size("blk")
    source = lax.axis_index("blk")
    part_index = lax.axis_index("feat")
    blocks_here, quarter, features = feat_a.shape
    link_count = owner_a.shape[1]
    tile_rows = tiles_a.shape[2]
    capacity_links = max(2, -(-blocks_here * link_count // peer_count))
    chosen_a, filled_a, slots_a = link_plan(owner_a, local_a, peer_count, capacity_links, source)
    chosen_b, filled_b, slots_b = link_plan(owner_b, local_b, peer_count, capacity_links, source)
    outgoing_a = outgoing_blocks(feat_a, chosen_a, filled_a)
    outgoing_b = outgoing_blocks(feat_b, chosen_b, filled_b)
    arrived_a = lax.all_to_all(outgoing_a, "blk", split_axis=0, concat_axis=0, tiled=True)
    arrived_b = lax.all_to_all(outgoing_b, "blk", split_axis=0, concat_axis=0, tiled=True)
    partial_a = aggregate(tiles_a, arrived_a, slots_a)
    partial_b = aggregate(tiles_b, arrived_b, slots_b)
    summed_a, summed_b = (
        lax.psum_scatter(partial_a, "feat", scatter_dimension=1, tiled=True),
        lax.psum_scatter(partial_b, "feat", scatter_dimension=1, tiled=True),
    )
    emb_a = embedding(feat_a, summed_a, weight)
    emb_b = embedding(feat_b, summed_b, weight)
    full_a = lax.all_gather(emb_a, "feat", axis=1, tiled=True)
    groups_here = blocks_here // GA
    cand_count = cand_owner.shape[1]
    group_rows = GA * tile_rows
    capacity_cands = max(2, -(-groups_here * cand_count // peer_count))
    chosen_c, filled_c, slots_c = link_plan(
        cand_owner, cand_local, peer_count, capacity_cands, source
    )
    outgoing_c = outgoing_blocks(emb_b, chosen_c, filled_c)
    arrived_c = lax.all_to_all(outgoing_c, "blk", split_axis=0, concat_axis=0, tiled=True)
    key_rows = jnp.take(arrived_c.reshape(-1, quarter, features), slots_c, axis=0)
    key_rows = key_rows.reshape(groups_here, cand_count * quarter, features)
    query_rows = full_a.reshape(groups_here, group_rows, features)
    wanted = target.reshape(groups_here, group_rows)
    column_ids = jnp.arange(cand_count, dtype=jnp.int32)[:, None] * tile_rows + part_index * quarter
    column_ids = (column_ids + jnp.arange(quarter, dtype=jnp.int32)[None, :]).reshape(-1)
    score_list = []
    local_top = []
    local_total = []
    for group in range(groups_here):
        scores = score_scale * jnp.einsum(
            "ad,cd->ac", query_rows[group], key_rows[group], preferred_element_type=jnp.float32
        )
        highest = jnp.max(scores, axis=1)
        score_list.append(scores)
        local_top.append(highest)
        local_total.append(jnp.sum(jnp.exp(scores - highest[:, None]), axis=1))
    local_top = jnp.stack(local_top)
    row_top = lax.pmax(local_top, "feat")
    partial_totals = jnp.stack(
        [
            jnp.sum(jnp.exp(score_list[group] - row_top[group][:, None]), axis=1)
            for group in range(groups_here)
        ]
    )
    row_total = lax.psum(partial_totals, "feat")
    query_terms = []
    key_terms = []
    for group in range(groups_here):
        probability = (
            jnp.exp(score_list[group] - row_top[group][:, None]) / row_total[group][:, None]
        )
        picked = (column_ids[None, :] == wanted[group][:, None]).astype(jnp.float32)
        dscore = (probability - picked).astype(jnp.bfloat16)
        query_terms.append(
            score_scale * jnp.dot(dscore, key_rows[group], preferred_element_type=jnp.float32)
        )
        key_terms.append(
            (
                score_scale
                * jnp.einsum(
                    "ac,ad->cd", dscore, query_rows[group], preferred_element_type=jnp.float32
                )
            ).astype(jnp.bfloat16)
        )
    query_stack = jnp.stack(query_terms).reshape(groups_here, GA, tile_rows, features)
    grad_a = lax.psum_scatter(query_stack, "feat", scatter_dimension=2, tiled=True).reshape(
        blocks_here, quarter, features
    )
    key_stack = jnp.stack(key_terms).reshape(groups_here * cand_count, quarter, features)
    return_buffer = (
        jnp.zeros((peer_count * capacity_cands, quarter, features), jnp.bfloat16)
        .at[slots_c]
        .set(key_stack)
    )
    returned = lax.all_to_all(
        return_buffer.reshape(peer_count, capacity_cands, quarter, features),
        "blk",
        split_axis=0,
        concat_axis=0,
        tiled=True,
    )
    owner_onehot = (
        jnp.arange(blocks_here, dtype=jnp.int32)[None, None, :] == chosen_c[:, :, None]
    ) & filled_c[:, :, None]
    grad_b = jnp.einsum(
        "psb,psrd->brd",
        owner_onehot.astype(jnp.float32),
        returned.astype(jnp.float32),
        precision=lax.Precision.HIGHEST,
    )
    return (grad_a, grad_b)


def solution(mesh):
    placed = (
        P("blk", "feat", None),
        P("blk", None, None, "feat"),
        P(),
        P(),
        P("blk", "feat", None),
        P("blk", None, None, "feat"),
        P(),
        P(),
        P(),
        P(),
        P(),
        P("blk", None),
    )
    return jax.shard_map(
        per_device,
        mesh=mesh,
        in_specs=placed,
        out_specs=(P("blk", "feat", None), P("blk", "feat", None)),
        check_vma=False,
    )
```

profile of v0, /device:TPU:8, one launch (start us, length us, event | category | flops | bytes accessed | tf_op | source)
XLA Modules:
  0.0 337.2 jit_solution(17975864941082551399)
XLA Ops:
  7.2 1.2 copy.58
  8.5 0.5 reshape.206
  9.0 0.3 copy.74
  9.3 0.5 reshape.214
  9.9 0.2 reduce_window_sum.35
  10.2 0.3 copy.78
  10.6 0.5 broadcast_in_dim.129
  11.9 0.8 gather_fusion.3
  12.6 2.3 select_select_fusion.1
  14.9 18.0 %all-to-all-start.1 = ((bf16[128,2,16,256]{3,2,1,0:T(8,128)(2,1)}), bf16[128,2,16,256]{3,2,1,0:T(8,128)(2,1)}, u32[]{:S(2)}, u32[]{:S(2)}) async-start(bf16[128,2,16,256]{3,2,1,0:T(8,128)(2,1)} %select_select_fusion.1), calls=%async_computation.2 | async-start | bytes 4194304 | tf_op jit(solution)/shard_map/all_to_all | solution.py:90
  33.3 0.3 copy.62
  33.6 0.5 broadcast_in_dim.122
  34.9 0.8 gather_fusion.1
  35.7 2.3 select_select_fusion.2
  38.0 48.6 %all-to-all-done.1 = bf16[128,2,16,256]{3,2,1,0:T(8,128)(2,1)} async-done(((bf16[128,2,16,256]{3,2,1,0:T(8,128)(2,1)}), bf16[128,2,16,256]{3,2,1,0:T(8,128)(2,1)}, u32[]{:S(2)}, u32[]{:S(2)}) %all-to-all-start.1) | async-done | bytes 2097184 | tf_op jit(solution)/shard_map/all_to_all | solution.py:90
  86.6 6.5 %all-to-all-start = ((bf16[128,2,16,256]{3,2,1,0:T(8,128)(2,1)}), bf16[128,2,16,256]{3,2,1,0:T(8,128)(2,1)}, u32[]{:S(2)}, u32[]{:S(2)}) async-start(bf16[128,2,16,256]{3,2,1,0:T(8,128)(2,1)} %select_select_fusion.2), calls=%async_computation | async-start | bytes 4194304 | tf_op jit(solution)/shard_map/all_to_all | solution.py:89
  93.4 2.2 gather_fusion.4
  95.6 0.2 broadcast_select_fusion.1
  95.8 1.4 convolution_bitcast_fusion
  99.1 0.4 copy-done.20
  99.4 27.7 %reduce-scatter.6.cloned.1.call-done = f32[16,16,256]{2,1,0:T(8,128)} async-done(((f32[16,64,256]{2,1,0:T(8,128)}), f32[16,16,256]{2,1,0:T(8,128)}) %reduce-scatter.6.cloned.1.call-update) | async-done | bytes 262160 | tf_op jit(solution)/shard_map/reduce_scatter | solution.py:95
  127.1 1.0 add_convert_fusion
  128.1 0.2 fusion.12
  128.3 0.8 gather_fusion.5
  129.1 2.3 select_select_fusion
  131.4 15.4 %all-to-all-done = bf16[128,2,16,256]{3,2,1,0:T(8,128)(2,1)} async-done(((bf16[128,2,16,256]{3,2,1,0:T(8,128)(2,1)}), bf16[128,2,16,256]{3,2,1,0:T(8,128)(2,1)}, u32[]{:S(2)}, u32[]{:S(2)}) %all-to-all-start) | async-done | bytes 2097184 | tf_op jit(solution)/shard_map/all_to_all | solution.py:89
  146.8 6.1 %all-to-all-start.2 = ((bf16[128,2,16,256]{3,2,1,0:T(8,128)(2,1)}), bf16[128,2,16,256]{3,2,1,0:T(8,128)(2,1)S(1)}, u32[]{:S(2)}, u32[]{:S(2)}) async-start(bf16[128,2,16,256]{3,2,1,0:T(8,128)(2,1)} %select_select_fusion), calls=%async_computation.4 | async-start | bytes 4194304 | tf_op jit(solution)/shard_map/all_to_all | solution.py:108
  153.1 3.3 gather_fusion.2
  156.4 1.4 broadcast_select_fusion.2
  157.8 1.3 convolution_bitcast_fusion.1
  159.4 0.7 fusion.35
  160.1 0.7 eq.179
  160.8 0.7 eq.182
  161.4 0.2 convert_reduce_fusion
  161.7 27.5 %reduce-scatter.4.cloned.1.call-done = f32[16,16,256]{2,1,0:T(8,128)} async-done(((f32[16,64,256]{2,1,0:T(8,128)}), f32[16,16,256]{2,1,0:T(8,128)}) %reduce-scatter.4.cloned.1.call-update) | async-done | bytes 262160 | tf_op jit(solution)/shard_map/reduce_scatter | solution.py:94
  189.1 1.0 add_convert_fusion.1
  190.1 0.2 fusion.11
  190.3 13.0 %all_gather.3 = bf16[16,64,256]{2,1,0:T(8,128)(2,1)S(1)} all-gather(bf16[16,16,256]{2,1,0:T(8,128)(2,1)S(1)} %bitcast.105), channel_id=1, replica_groups=mesh['blk'=128,'feat'=4] {'feat'}, dimensions={1}, use_global_device_ids=true | all-gather | bytes 655360 | tf_op jit(solution)/shard_map/all_gather | solution.py:99
  203.3 0.8 fusion.34
  204.2 2.7 all-to-all-done.2
  206.9 2.0 gather_fusion
  208.9 1.7 broadcast_select_fusion
  210.8 0.8 copy-done.8
  211.6 2.3 fusion.38
  213.9 2.3 fusion.39
  216.2 10.5 %pmax.7 = f32[2,512]{1,0:T(2,128)S(1)} all-reduce(f32[2,512]{1,0:T(2,128)S(1)} %pad_maximum_fusion.2), channel_id=1, replica_groups=mesh['blk'=128,'feat'=4] {'feat'}, use_global_device_ids=true, to_apply=%region_17.20 | all-reduce | flops 1024 | bytes 8192 | tf_op jit(solution)/shard_map/pmax | solution.py:127
  226.7 2.6 fusion
  229.3 0.2 copy-done.3
  229.5 0.6 fusion.1
  230.1 7.8 %psum.7 = f32[2,512]{1,0:T(2,128)S(1)} all-reduce(f32[2,512]{1,0:T(2,128)S(1)} %pad_maximum_fusion.3), channel_id=1, replica_groups=mesh['blk'=128,'feat'=4] {'feat'}, use_global_device_ids=true, to_apply=%region_20.23 | all-reduce | flops 1024 | bytes 8192 | tf_op jit(solution)/shard_map/psum | solution.py:134
  237.9 3.8 %subtract_convert_fusion.1 = (bf16[512,1536]{1,0:T(8,128)(2,1)S(1)}, bf16[512,1536]{1,0:T(8,128)(2,1)S(1)}) fusion(f32[512,1536]{1,0:T(8,128)} %get-tuple-element.35, s32[1536]{0:T(1024)S(1)} %add.134, f32[512]{0:T(512)S(1)} %bitcast.123, f32[512]{0:T(512)S(1)} %bitcast.114, s32[512]{0:T(512)S(1)} %copy-done.18, s32[512]{0:T(512)S(1)} %copy-done.19, ...), kind=kLoop, calls=%fused_computation.10 | loop fusion | flops 9437184 | bytes 9455616 | tf_op jit(solution)/shard_map/convert_element_type | solution.py:142
  241.7 0.6 fusion.5
  242.3 0.6 fusion.4
  242.9 0.4 copy-done.7
  243.3 1.3 pad_maximum_fusion
  244.8 14.3 %scatter_fusion = bf16[256,16,256]{2,1,0:T(8,128)(2,1)S(1)} fusion(bf16[256,16,256]{2,1,0:T(8,128)(2,1)S(1)} %broadcast_in_dim.135, s32[192]{0:T(256)S(1)} %bitcast.121, bf16[192,16,256]{2,1,0:T(8,128)(2,1)} %bitcast.93), kind=kCustom, calls=%fused_computation.6 | custom fusion | bytes 4719360 | tf_op jit(solution)/shard_map/scatter | solution.py:162
  259.1 3.8 %copy.82 = bf16[128,2,16,256]{3,1,2,0:T(2,128)(2,1)} copy(bf16[128,2,16,256]{3,2,1,0:T(8,128)(2,1)S(1)} %bitcast.88) | data formatting | bytes 4194304 | tf_op jit(solution)/shard_map/reshape | solution.py:165
  262.8 10.7 %all-to-all-start.3 = ((bf16[128,2,16,256]{3,1,2,0:T(2,128)(2,1)}), bf16[128,2,16,256]{3,1,2,0:T(2,128)(2,1)S(1)}, u32[]{:S(2)}, u32[]{:S(2)}) async-start(bf16[128,2,16,256]{3,1,2,0:T(2,128)(2,1)} %copy.82), calls=%async_computation.6 | async-start | bytes 4194304 | tf_op jit(solution)/shard_map/all_to_all | solution.py:164
  273.6 2.3 convolution_multiply_fusion.5
  275.9 0.6 convolution_multiply_fusion.4
  276.5 1.1 pad_maximum_fusion.1
  277.6 50.0 %all-to-all-done.3 = bf16[128,2,16,256]{3,1,2,0:T(2,128)(2,1)S(1)} async-done(((bf16[128,2,16,256]{3,1,2,0:T(2,128)(2,1)}), bf16[128,2,16,256]{3,1,2,0:T(2,128)(2,1)S(1)}, u32[]{:S(2)}, u32[]{:S(2)}) %all-to-all-start.3) | async-done | bytes 2097184 | tf_op jit(solution)/shard_map/all_to_all | solution.py:164
  327.6 2.3 fusion.8
  329.8 0.9 copy.84
  (119 shorter events, 5.0 us)
Async XLA Ops:
  7.2 88.7 %copy-start = (bf16[16,8,64,16]{2,3,1,0:T(8,128)(2,1)S(1)}, bf16[16,8,64,16]{2,3,1,0:T(8,128)(2,1)}, u32[]{:S(2)}) copy-start(bf16[16,8,64,16]{2,3,1,0:T(8,128)(2,1)} %param.21) | copy-start | bytes 786436
  7.2 1.8 copy-start.15
  8.4 1.8 copy-start.16
  9.3 2.6 copy-start.1
  14.9 18.4 %copy-start.17 = (s32[2048,8]{0,1:T(8,128)S(1)}, s32[2048,8]{0,1:T(8,128)}, u32[]{:S(2)}) copy-start(s32[2048,8]{0,1:T(8,128)} %param.19) | copy-start | bytes 196612
  14.9 71.7 %all-to-all-start.1 = ((bf16[128,2,16,256]{3,2,1,0:T(8,128)(2,1)}), bf16[128,2,16,256]{3,2,1,0:T(8,128)(2,1)}, u32[]{:S(2)}, u32[]{:S(2)}) async-start(bf16[128,2,16,256]{3,2,1,0:T(8,128)(2,1)} %select_select_fusion.1), calls=%async_computation.2 | async-start | bytes 4194304 | tf_op jit(solution)/shard_map/all_to_all | solution.py:90
  32.9 2.1 copy-start.2
  86.6 60.2 %all-to-all-start = ((bf16[128,2,16,256]{3,2,1,0:T(8,128)(2,1)}), bf16[128,2,16,256]{3,2,1,0:T(8,128)(2,1)}, u32[]{:S(2)}, u32[]{:S(2)}) async-start(bf16[128,2,16,256]{3,2,1,0:T(8,128)(2,1)} %select_select_fusion.2), calls=%async_computation | async-start | bytes 4194304 | tf_op jit(solution)/shard_map/all_to_all | solution.py:89
  93.1 34.0 %reduce-scatter.6.cloned.1.call-start = ((), (), s32[]{:S(2)}) async-start(), calls=%async_computation.8 | async-start | bytes 1310720 | tf_op jit(solution)/shard_map/reduce_scatter | solution.py:95
  95.8 1.4 copy-start.13
  97.2 0.9 copy-start.14
  97.2 30.9 %copy-start.11 = (bf16[256,256]{1,0:T(8,128)(2,1)S(1)}, bf16[256,256]{1,0:T(8,128)(2,1)}, u32[]{:S(2)}) copy-start(bf16[256,256]{1,0:T(8,128)(2,1)} %param.24) | copy-start | bytes 393220
  98.9 0.5 copy-start.20
  146.8 60.1 %all-to-all-start.2 = ((bf16[128,2,16,256]{3,2,1,0:T(8,128)(2,1)}), bf16[128,2,16,256]{3,2,1,0:T(8,128)(2,1)S(1)}, u32[]{:S(2)}, u32[]{:S(2)}) async-start(bf16[128,2,16,256]{3,2,1,0:T(8,128)(2,1)} %select_select_fusion), calls=%async_computation.4 | async-start | bytes 4194304 | tf_op jit(solution)/shard_map/all_to_all | solution.py:108
  152.9 36.3 %reduce-scatter.4.cloned.1.call-start = ((), (), s32[]{:S(2)}) async-start(), calls=%async_computation.7 | async-start | bytes 1310720 | tf_op jit(solution)/shard_map/reduce_scatter | solution.py:94
  153.1 4.7 %copy-start.10 = (bf16[16,8,64,16]{2,3,1,0:T(8,128)(2,1)S(1)}, bf16[16,8,64,16]{2,3,1,0:T(8,128)(2,1)}, u32[]{:S(2)}) copy-start(bf16[16,8,64,16]{2,3,1,0:T(8,128)(2,1)} %param.17) | copy-start | bytes 786436
  157.8 32.3 %copy-start.12 = (bf16[256,256]{1,0:T(8,128)(2,1)S(1)}, bf16[256,256]{1,0:T(8,128)(2,1)}, u32[]{:S(2)}) copy-start(bf16[256,256]{1,0:T(8,128)(2,1)} %param.24) | copy-start | bytes 393220
  210.6 1.0 copy-start.8
  210.7 3.1 copy-start.4
  211.6 2.3 copy-start.9
  226.7 2.8 copy-start.3
  229.3 8.6 %copy-start.18 = (s32[512]{0:T(512)S(1)}, s32[512]{0:T(512)}, u32[]{:S(2)}) copy-start(s32[512]{0:T(512)} %eq.179) | copy-start | bytes 6148
  229.3 8.6 %copy-start.19 = (s32[512]{0:T(512)S(1)}, s32[512]{0:T(512)}, u32[]{:S(2)}) copy-start(s32[512]{0:T(512)} %eq.182) | copy-start | bytes 6148
  241.6 1.3 copy-start.5
  241.7 1.7 copy-start.7
  262.8 64.7 %all-to-all-start.3 = ((bf16[128,2,16,256]{3,1,2,0:T(2,128)(2,1)}), bf16[128,2,16,256]{3,1,2,0:T(2,128)(2,1)S(1)}, u32[]{:S(2)}, u32[]{:S(2)}) async-start(bf16[128,2,16,256]{3,1,2,0:T(2,128)(2,1)} %copy.82), calls=%async_computation.6 | async-start | bytes 4194304 | tf_op jit(solution)/shard_map/all_to_all | solution.py:164
  273.5 57.2 %reduce-scatter.8.cloned.1.call-start = ((), (), s32[]{:S(2)}) async-start(), calls=%async_computation.9 | async-start | bytes 1310720 | tf_op jit(solution)/shard_map/reduce_scatter | solution.py:155
  273.5 2.3 copy-start.6
  276.4 51.1 %copy-start.21 = (pred[128,2]{0,1:T(4,128)(4,1)S(1)}, pred[128,2]{0,1:T(4,128)(4,1)}, u32[]{:S(2)}) copy-start(pred[128,2]{0,1:T(4,128)(4,1)} %copy-done.20) | copy-start | bytes 772
Sparse Core Ops, SparseCore 0:
  97.3 29.7 reduce-scatter.5
  159.3 29.7 reduce-scatter.3
  277.7 27.6 reduce-scatter.7
where the time goes:
time: 338 us; the launch traced here: 337 us
  waiting for transfers between devices  172 us (51%)
  starting transfers between devices  41.3 us (12%)
  local copies, waits for them, and re-layouts  40.8 us (12%)
  blocking collectives  31.3 us (9%)
  other arithmetic  23.3 us (7%)
  between operations  14.5 us (4%)
  matrix products  14.1 us (4%)
    all_to_all x1, waiting for transfers between devices, per_device(): lax.all_to_all(return_buffer.reshape(peer_count, capacity_cands, quarter,...  50 us
    all_to_all x1, waiting for transfers between devices, per_device(): lax.all_to_all(outgoing_b, 'blk', split_axis=0, concat_axis=0, tiled=True)  48.6 us
    reduce_scatter x1, waiting for transfers between devices, per_device(): lax.psum_scatter(partial_b, 'feat', scatter_dimension=1, tiled=True)  27.7 us
    reduce_scatter x1, waiting for transfers between devices, per_device(): lax.psum_scatter(partial_a, 'feat', scatter_dimension=1, tiled=True)  27.5 us
    all_to_all x1, starting transfers between devices, per_device(): lax.all_to_all(outgoing_b, 'blk', split_axis=0, concat_axis=0, tiled=True)  18 us
    all_to_all x1, waiting for transfers between devices, per_device(): lax.all_to_all(outgoing_a, 'blk', split_axis=0, concat_axis=0, tiled=True)  15.4 us
    scatter x1, local copies, waits for them, and re-layouts, per_device(): return_buffer = jnp.zeros((peer_count * capacity_cands, quarter, features...  14.3 us
    all_gather x1, blocking collectives, per_device(): full_a = lax.all_gather(emb_a, 'feat', axis=1, tiled=True)  13 us
  transfers between devices with their start and end apart: 7, of which 6 were waited for; matrix products, arithmetic and copies ran while one was open for 10% of the time, Pallas kernels for 0%

commit v1 on v0

v1 whole, which is shorter than its diff:
```python
import functools

import jax
import jax.numpy as jnp
from jax import lax
from jax.experimental import pallas as pl
from jax.experimental.pallas import tpu as pltpu
from jax.sharding import PartitionSpec as P

GA = 8
SPLITS = 4

score_scale = 0.25
hidden = -1e30


def link_sending(owner, within, peer_count, source):
    rows = owner.shape[0] // peer_count
    place = jnp.arange(rows * owner.shape[1], dtype=jnp.int32).reshape(1, rows, owner.shape[1])
    code = place * 16 + within.reshape(peer_count, rows, -1)
    present = owner.reshape(peer_count, rows, -1) == source
    first = jnp.min(jnp.where(present, code, 1 << 20), axis=(1, 2))
    last = jnp.max(jnp.where(present, code, 0), axis=(1, 2))
    return jnp.stack([first, last], axis=1).reshape(-1) & 15


def link_slots(owner, peer_count, source):
    own = lax.dynamic_index_in_dim(owner.reshape(peer_count, -1), source, 0, keepdims=False)
    count = own.shape[0]
    same = own[:, None] == own[None, :]
    before = jnp.arange(count)[None, :] < jnp.arange(count)[:, None]
    return own * 2 + jnp.any(same & before, axis=1).astype(jnp.int32)


def pick(rows, index):
    return jnp.take(rows, index, axis=0, mode="clip")


def exchange(rows, peer_count):
    blocks = rows.reshape(peer_count, 2, *rows.shape[1:])
    return lax.all_to_all(blocks, "blk", split_axis=0, concat_axis=0, tiled=True)


def aggregate(tile_set, arrived, slots):
    neighbours = pick(arrived.reshape(-1, *arrived.shape[2:]), slots)
    neighbours = neighbours.reshape(*tile_set.shape[:2], *arrived.shape[2:])
    return jnp.einsum("bkrc,bkcd->brd", tile_set, neighbours, preferred_element_type=jnp.float32)


def embedding(local_features, summed, weight):
    blocks, quarter, features = local_features.shape
    propagated = (
        (local_features.astype(jnp.float32) + summed)
        .astype(jnp.bfloat16)
        .reshape(blocks * quarter, features)
    )
    preact = jnp.dot(propagated, weight, preferred_element_type=jnp.float32)
    return jnp.maximum(preact, 0.0).astype(jnp.bfloat16).reshape(blocks, quarter, features)


def key_chunk(key_ref, step):
    owners = key_ref.shape[0] // SPLITS
    blocks = key_ref[pl.ds(step * owners, owners), 0]
    return blocks.reshape(owners * blocks.shape[1], blocks.shape[2])


def chunk_scores(keys, queries, bias):
    product = lax.dot_general(
        keys, queries, (((1,), (1,)), ((), ())), preferred_element_type=jnp.float32
    )
    return score_scale * product + bias


def stats_kernel(key_ref, query_ref, bias_ref, out_ref, score_ref):
    queries = query_ref[0]
    rows = score_ref.shape[0] // SPLITS
    top = None
    for step in range(SPLITS):
        part = pl.ds(step * rows, rows)
        scores = chunk_scores(key_chunk(key_ref, step), queries, bias_ref[0, part, :])
        score_ref[part, :] = scores
        highest = jnp.max(scores, axis=0, keepdims=True)
        top = highest if top is None else jnp.maximum(top, highest)
    total = jnp.zeros_like(top)
    for step in range(SPLITS):
        part = pl.ds(step * rows, rows)
        total = total + jnp.sum(jnp.exp(score_ref[part, :] - top), axis=0, keepdims=True)
    out_ref[0, 0:1, :] = top
    out_ref[0, 1:2, :] = total


def grads_kernel(key_ref, query_ref, bias_ref, stats_ref, wanted_ref, key_out, query_out):
    queries = query_ref[0]
    owners = key_ref.shape[0] // SPLITS
    rows = owners * key_ref.shape[2]
    tops = [stats_ref[part, 0, 0:1, :] for part in range(stats_ref.shape[0])]
    totals = [stats_ref[part, 0, 1:2, :] for part in range(stats_ref.shape[0])]
    top = functools.reduce(jnp.maximum, tops)
    denom = sum(total * jnp.exp(high - top) for high, total in zip(tops, totals))
    inverse = 1.0 / denom
    wanted = wanted_ref[0]
    gathered = None
    for step in range(SPLITS):
        keys = key_chunk(key_ref, step)
        scores = chunk_scores(keys, queries, bias_ref[0, pl.ds(step * rows, rows), :])
        probability = jnp.exp(scores - top) * inverse
        ids = lax.broadcasted_iota(jnp.int32, probability.shape, 0) + step * rows
        dscore = jnp.where(ids == wanted, probability - 1.0, probability).astype(jnp.bfloat16)
        key_term = score_scale * jnp.dot(dscore, queries, preferred_element_type=jnp.float32)
        key_out[pl.ds(step * owners, owners), 0] = key_term.astype(jnp.bfloat16).reshape(
            owners, key_ref.shape[2], key_ref.shape[3]
        )
        piece = lax.dot_general(
            dscore, keys, (((0,), (0,)), ((), ())), preferred_element_type=jnp.float32
        )
        gathered = piece if gathered is None else gathered + piece
    query_out[0] = score_scale * gathered


def score_specs(keys, queries):
    peers, groups, quarter, features = keys.shape
    rows = queries.shape[1]
    return (
        pl.BlockSpec((peers, 1, quarter, features), lambda g: (0, g, 0, 0)),
        pl.BlockSpec((1, rows, features), lambda g: (g, 0, 0)),
        pl.BlockSpec((1, peers * quarter, 1), lambda g: (g, 0, 0)),
    )


def score_stats(keys, queries, bias):
    peers, groups, quarter, features = keys.shape
    rows = queries.shape[1]
    return pl.pallas_call(
        stats_kernel,
        grid=(groups,),
        in_specs=score_specs(keys, queries),
        out_specs=pl.BlockSpec((1, 2, rows), lambda g: (g, 0, 0)),
        out_shape=jax.ShapeDtypeStruct((groups, 2, rows), jnp.float32),
        scratch_shapes=[pltpu.VMEM((peers * quarter, rows), jnp.float32)],
        compiler_params=pltpu.CompilerParams(vmem_limit_bytes=32 << 20),
        name="score_stats",
    )(keys, queries, bias)


def score_grads(keys, queries, bias, stats, wanted):
    peers, groups, quarter, features = keys.shape
    rows = queries.shape[1]
    key_spec, query_spec, bias_spec = score_specs(keys, queries)
    return pl.pallas_call(
        grads_kernel,
        grid=(groups,),
        in_specs=(
            key_spec,
            query_spec,
            bias_spec,
            pl.BlockSpec((stats.shape[0], 1, 2, rows), lambda g: (0, g, 0, 0)),
            pl.BlockSpec((1, 1, rows), lambda g: (g, 0, 0)),
        ),
        out_specs=(key_spec, query_spec),
        out_shape=(
            jax.ShapeDtypeStruct(keys.shape, jnp.bfloat16),
            jax.ShapeDtypeStruct(queries.shape, jnp.float32),
        ),
        compiler_params=pltpu.CompilerParams(vmem_limit_bytes=32 << 20),
        name="score_grads",
    )(keys, queries, bias, stats, wanted)


def per_device(
    feat_a,
    tiles_a,
    owner_a,
    local_a,
    feat_b,
    tiles_b,
    owner_b,
    local_b,
    weight,
    cand_owner,
    cand_local,
    target,
):
    peer_count = lax.axis_size("blk")
    source = lax.axis_index("blk")
    part_index = lax.axis_index("feat")
    blocks_here, quarter, features = feat_a.shape
    tile_rows = tiles_a.shape[2]
    groups_here = blocks_here // GA
    group_rows = GA * tile_rows

    arrived_b = exchange(pick(feat_b, link_sending(owner_b, local_b, peer_count, source)), peer_count)
    arrived_a = exchange(pick(feat_a, link_sending(owner_a, local_a, peer_count, source)), peer_count)
    partial_b = aggregate(tiles_b, arrived_b, link_slots(owner_b, peer_count, source))
    partial_a = aggregate(tiles_a, arrived_a, link_slots(owner_a, peer_count, source))
    summed_b = lax.psum_scatter(partial_b, "feat", scatter_dimension=1, tiled=True)
    summed_a = lax.psum_scatter(partial_a, "feat", scatter_dimension=1, tiled=True)
    emb_b = embedding(feat_b, summed_b, weight)
    emb_a = embedding(feat_a, summed_a, weight)
    full_a = lax.all_gather(emb_a, "feat", axis=1, tiled=True)
    queries = full_a.reshape(groups_here, group_rows, features)

    named = cand_owner == source
    chosen = jnp.sum(jnp.where(named, cand_local, 0), axis=1)
    filled = jnp.any(named, axis=1)
    keys = exchange(pick(emb_b, chosen), peer_count)

    own = lax.dynamic_slice_in_dim(cand_owner, source * groups_here, groups_here, 0)
    peers = jnp.arange(peer_count, dtype=jnp.int32)
    arrives = jnp.any(own[:, :, None] == peers[None, None, :], axis=1)
    bias = jnp.where(jnp.repeat(arrives, quarter, axis=1), 0.0, hidden).astype(jnp.float32)[:, :, None]
    wanted = target.reshape(groups_here, group_rows)
    column = wanted // tile_rows
    row = wanted % tile_rows
    listed = jnp.arange(cand_owner.shape[1], dtype=jnp.int32)
    holder = jnp.sum(
        jnp.where(column[:, :, None] == listed[None, None, :], own[:, None, :], 0), axis=2
    )
    inside = row // quarter == part_index
    wanted = jnp.where(inside, holder * quarter + row % quarter, -1)[:, None, :]

    stats = lax.all_gather(score_stats(keys, queries, bias), "feat", axis=0)
    key_terms, query_terms = score_grads(keys, queries, bias, stats, wanted)

    query_terms = query_terms.reshape(groups_here, GA, tile_rows, features)
    grad_a = lax.psum_scatter(query_terms, "feat", scatter_dimension=2, tiled=True).reshape(
        blocks_here, quarter, features
    )
    returned = lax.all_to_all(key_terms, "blk", split_axis=0, concat_axis=0, tiled=True)
    holds = (jnp.arange(blocks_here, dtype=jnp.int32)[None, :] == chosen[:, None]) & filled[:, None]
    grad_b = jnp.einsum(
        "sb,srd->brd",
        holds.astype(jnp.bfloat16),
        returned.reshape(-1, quarter, features),
        preferred_element_type=jnp.float32,
    )
    return (grad_a, grad_b)


def solution(mesh):
    placed = (
        P("blk", "feat", None),
        P("blk", None, None, "feat"),
        P(),
        P(),
        P("blk", "feat", None),
        P("blk", None, None, "feat"),
        P(),
        P(),
        P(),
        P(),
        P(),
        P("blk", None),
    )
    return jax.shard_map(
        per_device,
        mesh=mesh,
        in_specs=placed,
        out_specs=(P("blk", "feat", None), P("blk", "feat", None)),
        check_vma=False,
    )
```

time: 338 us -> 304 us (0.90)
  other arithmetic: 23.3 us -> 4.99 us
  local copies, waits for them, and re-layouts: 40.8 us -> 29.5 us
  Pallas kernels: 0 us -> 9.12 us
  matrix products: 14.1 us -> 6.2 us
  blocking collectives: 31.3 us -> 25.4 us
    scatter x1 -> x0, local copies, waits for them, and re-layouts: 14.3 us -> none  [per_device(): return_buffer = jnp.zeros((peer_count * capacity_cands, quarter, features...]
    all_gather x0 -> x1, blocking collectives: none -> 12.3 us  [per_device(): stats = lax.all_gather(score_stats(keys, queries, bias), 'feat', axis=0)]
    pmax x1 -> x0, blocking collectives: 10.5 us -> none  [per_device(): row_top = lax.pmax(local_top, 'feat')]
    dot_general x7 -> x1, matrix products: 11 us -> 0.67 us  [per_device(): jnp.einsum('sb,srd->brd', holds.astype(jnp.bfloat16), returned.reshape(-1...]
    select_n x10 -> x3, other arithmetic: 10.2 us -> 0.07 us  [the longest x1 0.05 us: per_device(): wanted = jnp.where(inside, holder * quarter + row % quarter, -1)[:, None, :]]
    pallas_call x0 -> x2, Pallas kernels: none -> 9.12 us  [the longest x1 6.05 us: score_grads(): pl.pallas_call(grads_kernel, grid=(groups,), in_specs=(key_spec, query_sp...]
    psum x1 -> x0, blocking collectives: 7.75 us -> none  [per_device(): row_total = lax.psum(partial_totals, 'feat')]
    unnamed x52 -> x33, local copies, waits for them, and re-layouts: 5.3 us -> 9.55 us
where the time goes in v1:
time: 304 us; the launch traced here: 303 us
  waiting for transfers between devices  173 us (57%)
  starting transfers between devices  40.6 us (13%)
  local copies, waits for them, and re-layouts  29.5 us (10%)
  blocking collectives  25.4 us (8%)
  between operations  14.1 us (5%)
  Pallas kernels  9.12 us (3%)
  matrix products  6.2 us (2%)
  other arithmetic  4.99 us (2%)
    all_to_all x3, waiting for transfers between devices, exchange(): lax.all_to_all(blocks, 'blk', split_axis=0, concat_axis=0, tiled=True)  62.6 us
    all_to_all x1, waiting for transfers between devices, per_device(): lax.all_to_all(key_terms, 'blk', split_axis=0, concat_axis=0, tiled=True)  53.3 us
    reduce_scatter x1, waiting for transfers between devices, per_device(): lax.psum_scatter(partial_b, 'feat', scatter_dimension=1, tiled=True)  29.8 us
    all_to_all x3, starting transfers between devices, exchange(): lax.all_to_all(blocks, 'blk', split_axis=0, concat_axis=0, tiled=True)  29.6 us
    reduce_scatter x1, waiting for transfers between devices, per_device(): lax.psum_scatter(partial_a, 'feat', scatter_dimension=1, tiled=True)  26.7 us
    all_gather x1, blocking collectives, per_device(): full_a = lax.all_gather(emb_a, 'feat', axis=1, tiled=True)  13.2 us
    gather x5, local copies, waits for them, and re-layouts, pick(): return jnp.take(rows, index, axis=0, mode='clip')  12.7 us
    all_gather x1, blocking collectives, per_device(): stats = lax.all_gather(score_stats(keys, queries, bias), 'feat', axis=0)  12.3 us
  transfers between devices with their start and end apart: 7, of which 6 were waited for; matrix products, arithmetic and copies ran while one was open for 10% of the time, Pallas kernels for 0%

profile of v1, /device:TPU:8, one launch (start us, length us, event | category | flops | bytes accessed | tf_op | source)
XLA Modules:
  0.0 303.1 jit_solution(17140618703534666107)
XLA Ops:
  7.3 0.3 add.118
  7.5 1.1 select_reduce_fusion.3
  8.6 0.1 reduce_min.24
  8.7 0.1 reduce_max.24
  8.7 0.1 reduce_min.25
  8.9 0.1 reduce_max.25
  9.0 0.1 copy.38
  9.1 0.1 reshape.380
  9.3 2.0 gather_fusion
  11.3 17.5 %all-to-all-start = ((bf16[128,2,16,256]{3,2,1,0:T(8,128)(2,1)}), bf16[128,2,16,256]{3,2,1,0:T(8,128)(2,1)S(1)}, u32[]{:S(2)}, u32[]{:S(2)}) async-start(bf16[128,2,16,256]{3,2,1,0:T(8,128)(2,1)} %bitcast.2), calls=%async_computation | async-start | bytes 4194304 | tf_op jit(solution)/shard_map/all_to_all | solution.py:41
  28.8 0.1 reduce_min.36
  28.9 0.1 reduce_min.37
  29.0 0.1 reduce_max.36
  29.1 0.1 reduce_max.37
  29.2 0.1 copy.40
  29.4 0.1 reshape.404
  29.5 2.1 gather_fusion.3
  31.6 51.2 %all-to-all-done = bf16[128,2,16,256]{3,2,1,0:T(8,128)(2,1)S(1)} async-done(((bf16[128,2,16,256]{3,2,1,0:T(8,128)(2,1)}), bf16[128,2,16,256]{3,2,1,0:T(8,128)(2,1)S(1)}, u32[]{:S(2)}, u32[]{:S(2)}) %all-to-all-start) | async-done | bytes 2097184 | tf_op jit(solution)/shard_map/all_to_all | solution.py:41
  82.9 1.3 copy-done.6
  84.2 6.1 %all-to-all-start.2 = ((bf16[128,2,16,256]{3,2,1,0:T(8,128)(2,1)}), bf16[128,2,16,256]{3,2,1,0:T(8,128)(2,1)S(1)}, u32[]{:S(2)}, u32[]{:S(2)}) async-start(bf16[128,2,16,256]{3,2,1,0:T(8,128)(2,1)} %bitcast.17), calls=%async_computation.3 | async-start | bytes 4194304 | tf_op jit(solution)/shard_map/all_to_all | solution.py:41
  90.2 0.0 reduce-scatter.4.cloned.1.call-start
  90.3 1.3 copy.39
  91.6 1.4 copy.41
  93.0 1.6 reshape.359
  94.6 1.6 reshape.366
  96.3 0.2 fusion.7
  96.5 0.4 copy-done.13
  96.9 3.2 %gather_fusion.1 = bf16[128,16,256]{2,1,0:T(8,128)(2,1)} fusion(bf16[256,16,256]{2,1,0:T(8,128)(2,1)} %bitcast.70, s32[1024]{0:T(1024)S(1)} %pad_clamp_fusion.3), kind=kCustom, calls=%fused_computation.1 | custom fusion | bytes 2097664 | tf_op jit(solution)/shard_map/jit(_take)/gather | solution.py:36
  100.1 2.6 convolution_bitcast_fusion.1
  102.9 29.8 %reduce-scatter.4.cloned.1.call-done = f32[16,16,256]{2,1,0:T(8,128)} async-done(((f32[16,64,256]{2,1,0:T(8,128)}), f32[16,16,256]{2,1,0:T(8,128)}) %reduce-scatter.4.cloned.1.call-update) | async-done | bytes 262160 | tf_op jit(solution)/shard_map/reduce_scatter | solution.py:195
  132.7 1.0 add_convert_fusion.1
  133.7 0.2 fusion.2
  133.9 2.0 gather_fusion.2
  135.9 8.4 %all-to-all-done.2 = bf16[128,2,16,256]{3,2,1,0:T(8,128)(2,1)S(1)} async-done(((bf16[128,2,16,256]{3,2,1,0:T(8,128)(2,1)}), bf16[128,2,16,256]{3,2,1,0:T(8,128)(2,1)S(1)}, u32[]{:S(2)}, u32[]{:S(2)}) %all-to-all-start.2) | async-done | bytes 2097184 | tf_op jit(solution)/shard_map/all_to_all | solution.py:41
  144.3 1.3 copy-done.5
  145.7 6.1 %all-to-all-start.1 = ((bf16[128,2,16,256]{3,2,1,0:T(8,128)(2,1)}), bf16[128,2,16,256]{3,2,1,0:T(8,128)(2,1)S(1)}, u32[]{:S(2)}, u32[]{:S(2)}) async-start(bf16[128,2,16,256]{3,2,1,0:T(8,128)(2,1)} %bitcast.67), calls=%async_computation.2 | async-start | bytes 4194304 | tf_op jit(solution)/shard_map/all_to_all | solution.py:41
  151.8 0.2 fusion.8
  152.0 0.7 fusion.16
  152.7 3.2 %gather_fusion.4 = bf16[128,16,256]{2,1,0:T(8,128)(2,1)} fusion(bf16[256,16,256]{2,1,0:T(8,128)(2,1)} %bitcast.69, s32[1024]{0:T(1024)S(1)} %pad_clamp_fusion), kind=kCustom, calls=%fused_computation.4 | custom fusion | bytes 2097664 | tf_op jit(solution)/shard_map/jit(_take)/gather | solution.py:36
  155.9 2.6 convolution_bitcast_fusion
  158.5 0.1 reshape.372
  158.6 0.1 reshape.371
  158.7 0.1 constant_dynamic-slice_fusion
  158.8 0.1 copy.42
  158.8 0.1 fusion.4
  159.0 0.1 broadcast_in_dim.71
  159.1 2.5 select_n.118.bias_ref
  161.6 0.1 select_reduce_fusion
  161.7 0.1 compare_select_fusion.2.wanted_ref
  161.8 26.7 %reduce-scatter.6.cloned.1.call-done = f32[16,16,256]{2,1,0:T(8,128)} async-done(((f32[16,64,256]{2,1,0:T(8,128)}), f32[16,16,256]{2,1,0:T(8,128)}) %reduce-scatter.6.cloned.1.call-update) | async-done | bytes 262160 | tf_op jit(solution)/shard_map/reduce_scatter | solution.py:196
  188.5 1.0 add_convert_fusion
  189.4 0.2 fusion.3
  189.6 13.2 %all_gather.9 = bf16[16,64,256]{2,1,0:T(8,128)(2,1)S(1)} all-gather(bf16[16,16,256]{2,1,0:T(8,128)(2,1)S(1)} %bitcast.73), channel_id=1, replica_groups=mesh['blk'=128,'feat'=4] {'feat'}, dimensions={1}, use_global_device_ids=true | all-gather | bytes 655360 | tf_op jit(solution)/shard_map/all_gather | solution.py:199
  202.8 3.0 all-to-all-done.1.key_ref
  205.8 1.6 copy-done.1
  207.4 3.1 %score_stats.1 = f32[2,2,512]{2,1,0:T(2,128)S(1)} custom-call(bf16[128,2,16,256]{3,2,1,0:T(8,128)(2,1)S(1)} %all-to-all-done.1.key_ref, bf16[2,512,256]{2,1,0:T(8,128)(2,1)S(1)} %bitcast.63, f32[2,2048,1]{2,1,0:T(8,128)S(1)} %copy-done.1), custom_call_target="tpu_custom_call" | custom-call | tf_op jit(solution)/shard_map/score_stats/pallas_call | solution.py:133
  210.5 12.3 %all-gather = f32[8,2,512]{2,1,0:T(2,128)S(1)} all-gather(f32[2,2,512]{2,1,0:T(2,128)S(1)} %score_stats.1), channel_id=2, replica_groups=mesh['blk'=128,'feat'=4] {'feat'}, dimensions={0}, use_global_device_ids=true | all-gather | bytes 40960 | tf_op jit(solution)/shard_map/all_gather | solution.py:221
  222.7 6.0 %score_grads.1 = (bf16[128,2,16,256]{3,2,1,0:T(8,128)(2,1)S(1)}, f32[2,512,256]{2,1,0:T(8,128)}) custom-call(bf16[128,2,16,256]{3,2,1,0:T(8,128)(2,1)S(1)} %all-to-all-done.1.key_ref, bf16[2,512,256]{2,1,0:T(8,128)(2,1)S(1)} %bitcast.64, f32[2,2048,1]{2,1,0:T(8,128)S(1)} %copy-done.1, f32[4,2,2,512]{3,2,1,0:T(2,128)S(1)} %bitcast.65, ...), custom_call_target="tpu_custom_call" | custom-call | tf_op jit(solution)/shard_map/score_grads/pallas_call | solution.py:149
  228.8 1.3 copy-done.2
  230.1 10.8 %all-to-all-start.3 = ((bf16[128,2,16,256]{3,2,1,0:T(8,128)(2,1)}), bf16[128,2,16,256]{3,2,1,0:T(8,128)(2,1)S(1)}, u32[]{:S(2)}, u32[]{:S(2)}) async-start(bf16[128,2,16,256]{3,2,1,0:T(8,128)(2,1)} %copy-done.2), calls=%async_computation.6 | async-start | bytes 4194304 | tf_op jit(solution)/shard_map/all_to_all | solution.py:228
  241.0 0.7 reduce-scatter.8.cloned.1.call-update
  241.7 53.3 %all-to-all-done.3 = bf16[128,2,16,256]{3,2,1,0:T(8,128)(2,1)S(1)} async-done(((bf16[128,2,16,256]{3,2,1,0:T(8,128)(2,1)}), bf16[128,2,16,256]{3,2,1,0:T(8,128)(2,1)S(1)}, u32[]{:S(2)}, u32[]{:S(2)}) %all-to-all-start.3) | async-done | bytes 2097184 | tf_op jit(solution)/shard_map/all_to_all | solution.py:228
  295.0 0.7 fusion
  295.7 0.9 copy.47
  (46 shorter events, 0.4 us)
Async XLA Ops:
  7.2 93.0 %copy-start = (bf16[16,8,64,16]{2,3,1,0:T(8,128)(2,1)S(1)}, bf16[16,8,64,16]{2,3,1,0:T(8,128)(2,1)}, u32[]{:S(2)}) copy-start(bf16[16,8,64,16]{2,3,1,0:T(8,128)(2,1)} %param.17) | copy-start | bytes 786436
  7.2 2.1 copy-start.3
  11.3 18.2 %copy-start.4 = (bf16[16,16,256]{2,1,0:T(8,128)(2,1)S(1)}, bf16[16,16,256]{2,1,0:T(8,128)(2,1)}, u32[]{:S(2)}) copy-start(bf16[16,16,256]{2,1,0:T(8,128)(2,1)} %param.12) | copy-start | bytes 393220
  11.3 71.6 %all-to-all-start = ((bf16[128,2,16,256]{3,2,1,0:T(8,128)(2,1)}), bf16[128,2,16,256]{3,2,1,0:T(8,128)(2,1)S(1)}, u32[]{:S(2)}, u32[]{:S(2)}) async-start(bf16[128,2,16,256]{3,2,1,0:T(8,128)(2,1)} %bitcast.2), calls=%async_computation | async-start | bytes 4194304 | tf_op jit(solution)/shard_map/all_to_all | solution.py:41
  82.9 1.3 copy-start.6
  82.9 7.4 %copy-start.9 = (s32[2048,8]{0,1:T(8,128)S(1)}, s32[2048,8]{0,1:T(8,128)}, u32[]{:S(2)}) copy-start(s32[2048,8]{0,1:T(8,128)} %param.18) | copy-start | bytes 196612
  82.9 8.7 %copy-start.10 = (s32[2048,8]{0,1:T(8,128)S(1)}, s32[2048,8]{0,1:T(8,128)}, u32[]{:S(2)}) copy-start(s32[2048,8]{0,1:T(8,128)} %param.14) | copy-start | bytes 196612
  84.2 60.1 %all-to-all-start.2 = ((bf16[128,2,16,256]{3,2,1,0:T(8,128)(2,1)}), bf16[128,2,16,256]{3,2,1,0:T(8,128)(2,1)S(1)}, u32[]{:S(2)}, u32[]{:S(2)}) async-start(bf16[128,2,16,256]{3,2,1,0:T(8,128)(2,1)} %bitcast.17), calls=%async_computation.3 | async-start | bytes 4194304 | tf_op jit(solution)/shard_map/all_to_all | solution.py:41
  90.2 42.4 %reduce-scatter.4.cloned.1.call-start = ((), (), s32[]{:S(2)}) async-start(), calls=%async_computation.7 | async-start | bytes 1310720 | tf_op jit(solution)/shard_map/reduce_scatter | solution.py:195
  96.3 0.6 copy-start.13
  100.1 2.6 copy-start.11
  100.1 2.7 copy-start.12
  100.1 33.5 %copy-start.8 = (bf16[256,256]{1,0:T(8,128)(2,1)S(1)}, bf16[256,256]{1,0:T(8,128)(2,1)}, u32[]{:S(2)}) copy-start(bf16[256,256]{1,0:T(8,128)(2,1)} %param.20) | copy-start | bytes 393220
  144.3 1.4 copy-start.5
  145.7 60.1 %all-to-all-start.1 = ((bf16[128,2,16,256]{3,2,1,0:T(8,128)(2,1)}), bf16[128,2,16,256]{3,2,1,0:T(8,128)(2,1)S(1)}, u32[]{:S(2)}, u32[]{:S(2)}) async-start(bf16[128,2,16,256]{3,2,1,0:T(8,128)(2,1)} %bitcast.67), calls=%async_computation.2 | async-start | bytes 4194304 | tf_op jit(solution)/shard_map/all_to_all | solution.py:41
  151.7 4.2 %copy-start.7 = (bf16[16,8,64,16]{2,3,1,0:T(8,128)(2,1)S(1)}, bf16[16,8,64,16]{2,3,1,0:T(8,128)(2,1)}, u32[]{:S(2)}) copy-start(bf16[16,8,64,16]{2,3,1,0:T(8,128)(2,1)} %param.13) | copy-start | bytes 786436
  151.7 36.7 %reduce-scatter.6.cloned.1.call-start = ((), (), s32[]{:S(2)}) async-start(), calls=%async_computation.8 | async-start | bytes 1310720 | tf_op jit(solution)/shard_map/reduce_scatter | solution.py:196
  155.9 2.6 copy-start.14
  205.8 1.6 copy-start.1
  228.8 1.4 copy-start.2
  230.1 64.9 %all-to-all-start.3 = ((bf16[128,2,16,256]{3,2,1,0:T(8,128)(2,1)}), bf16[128,2,16,256]{3,2,1,0:T(8,128)(2,1)S(1)}, u32[]{:S(2)}, u32[]{:S(2)}) async-start(bf16[128,2,16,256]{3,2,1,0:T(8,128)(2,1)} %copy-done.2), calls=%async_computation.6 | async-start | bytes 4194304 | tf_op jit(solution)/shard_map/all_to_all | solution.py:228
  241.0 55.6 %reduce-scatter.8.cloned.1.call-start = ((), (), s32[]{:S(2)}) async-start(), calls=%async_computation.9 | async-start | bytes 1310720 | tf_op jit(solution)/shard_map/reduce_scatter | solution.py:225
Sparse Core Ops, SparseCore 0:
  102.9 29.7 reduce-scatter.3
  158.6 29.7 reduce-scatter.5
  245.2 28.1 reduce-scatter.7

commit v2 on v1

--- a/solution.py
+++ b/solution.py
@@ -56,6 +56,36 @@
     )
     preact = jnp.dot(propagated, weight, preferred_element_type=jnp.float32)
     return jnp.maximum(preact, 0.0).astype(jnp.bfloat16).reshape(blocks, quarter, features)
+
+
+def scatter_sum(partial, part_index, parts):
+    blocks, rows, features = partial.shape
+    pieces = partial.reshape(blocks, parts, rows // parts, features)
+    total = lax.dynamic_index_in_dim(pieces, part_index, 1, keepdims=False)
+    for shift in range(1, parts):
+        piece = lax.dynamic_index_in_dim(pieces, (part_index + shift) % parts, 1, keepdims=False)
+        moves = [(i, (i + shift) % parts) for i in range(parts)]
+        total = total + lax.ppermute(piece, "feat", moves)
+    return total
+
+
+def gather_rows(quarter_rows, part_index, parts):
+    blocks, quarter, features = quarter_rows.shape
+    held = [quarter_rows]
+    for shift in range(1, parts):
+        moves = [(i, (i + shift) % parts) for i in range(parts)]
+        held.append(lax.ppermute(quarter_rows, "feat", moves))
+    back = (part_index - jnp.arange(parts, dtype=jnp.int32)) % parts
+    ordered = pick(jnp.stack(held), back)
+    return jnp.moveaxis(ordered, 0, 1).reshape(blocks, parts * quarter, features)
+
+
+def collect_stats(stats, parts):
+    held = stats[None]
+    for flip in (1, 3):
+        moves = [(i, i ^ flip) for i in range(parts)]
+        held = jnp.concatenate([held, lax.ppermute(held, "feat", moves)], axis=0)
+    return held
 
 
 def key_chunk(key_ref, step):
@@ -183,6 +213,7 @@
     peer_count = lax.axis_size("blk")
     source = lax.axis_index("blk")
     part_index = lax.axis_index("feat")
+    parts = lax.axis_size("feat")
     blocks_here, quarter, features = feat_a.shape
     tile_rows = tiles_a.shape[2]
     groups_here = blocks_here // GA
@@ -192,11 +223,11 @@
     arrived_a = exchange(pick(feat_a, link_sending(owner_a, local_a, peer_count, source)), peer_count)
     partial_b = aggregate(tiles_b, arrived_b, link_slots(owner_b, peer_count, source))
     partial_a = aggregate(tiles_a, arrived_a, link_slots(owner_a, peer_count, source))
-    summed_b = lax.psum_scatter(partial_b, "feat", scatter_dimension=1, tiled=True)
-    summed_a = lax.psum_scatter(partial_a, "feat", scatter_dimension=1, tiled=True)
+    summed_b = scatter_sum(partial_b, part_index, parts)
+    summed_a = scatter_sum(partial_a, part_index, parts)
     emb_b = embedding(feat_b, summed_b, weight)
     emb_a = embedding(feat_a, summed_a, weight)
-    full_a = lax.all_gather(emb_a, "feat", axis=1, tiled=True)
+    full_a = gather_rows(emb_a, part_index, parts)
     queries = full_a.reshape(groups_here, group_rows, features)
 
     named = cand_owner == source
@@ -218,13 +249,11 @@
     inside = row // quarter == part_index
     wanted = jnp.where(inside, holder * quarter + row % quarter, -1)[:, None, :]
 
-    stats = lax.all_gather(score_stats(keys, queries, bias), "feat", axis=0)
+    stats = collect_stats(score_stats(keys, queries, bias), parts)
     key_terms, query_terms = score_grads(keys, queries, bias, stats, wanted)
 
-    query_terms = query_terms.reshape(groups_here, GA, tile_rows, features)
-    grad_a = lax.psum_scatter(query_terms, "feat", scatter_dimension=2, tiled=True).reshape(
-        blocks_here, quarter, features
-    )
+    query_terms = query_terms.reshape(blocks_here, tile_rows, features)
+    grad_a = scatter_sum(query_terms, part_index, parts)
     returned = lax.all_to_all(key_terms, "blk", split_axis=0, concat_axis=0, tiled=True)
     holds = (jnp.arange(blocks_here, dtype=jnp.int32)[None, :] == chosen[:, None]) & filled[:, None]
     grad_b = jnp.einsum(

time: 304 us -> 295 us (0.970)
  starting transfers between devices: 40.6 us -> 90.8 us
  waiting for transfers between devices: 173 us -> 136 us
  blocking collectives: 25.4 us -> 0 us
  between operations: 14.1 us -> 1.26 us
  local copies, waits for them, and re-layouts: 29.5 us -> 40.5 us
  other arithmetic: 4.99 us -> 10.8 us
    reduce_scatter x3 -> x0, waiting for transfers between devices: 56.5 us -> none  [the longest x1 29.8 us: per_device(): lax.psum_scatter(partial_b, 'feat', scatter_dimension=1, tiled=True)]
    ppermute x0 -> x14, starting transfers between devices: none -> 50 us  [the longest x9 31.1 us: scatter_sum(): total = total + lax.ppermute(piece, 'feat', moves)]
    ppermute x0 -> x14, waiting for transfers between devices: none -> 28.1 us  [the longest x9 23 us: scatter_sum(): total = total + lax.ppermute(piece, 'feat', moves)]
    all_gather x2 -> x0, blocking collectives: 25.4 us -> none  [the longest x1 13.2 us: per_device(): full_a = lax.all_gather(emb_a, 'feat', axis=1, tiled=True)]
    all_to_all x1, waiting for transfers between devices: 53.3 us -> 34.6 us  [per_device(): lax.all_to_all(key_terms, 'blk', split_axis=0, concat_axis=0, tiled=True)]
    all_to_all x3, waiting for transfers between devices: 62.6 us -> 73.8 us  [exchange(): lax.all_to_all(blocks, 'blk', split_axis=0, concat_axis=0, tiled=True)]
    unnamed x33 -> x53, local copies, waits for them, and re-layouts: 9.55 us -> 14.2 us
    gather x5 -> x6, local copies, waits for them, and re-layouts: 12.7 us -> 14.1 us  [pick(): return jnp.take(rows, index, axis=0, mode='clip')]
  transfers between devices with their start and end apart: 7 -> 18, of which waited for: 6 -> 13; matrix products, arithmetic and copies ran while one was open for 10% -> 13% of each run, Pallas kernels for 0% -> 0%
where the time goes in v2:
time: 295 us; the launch traced here: 294 us
  waiting for transfers between devices  136 us (46%)
  starting transfers between devices  90.8 us (31%)
  local copies, waits for them, and re-layouts  40.5 us (14%)
  other arithmetic  10.8 us (4%)
  Pallas kernels  8.25 us (3%)
  matrix products  5.82 us (2%)
    all_to_all x3, waiting for transfers between devices, exchange(): lax.all_to_all(blocks, 'blk', split_axis=0, concat_axis=0, tiled=True)  73.8 us
    all_to_all x1, waiting for transfers between devices, per_device(): lax.all_to_all(key_terms, 'blk', split_axis=0, concat_axis=0, tiled=True)  34.6 us
    ppermute x9, starting transfers between devices, scatter_sum(): total = total + lax.ppermute(piece, 'feat', moves)  31.1 us
    all_to_all x3, starting transfers between devices, exchange(): lax.all_to_all(blocks, 'blk', split_axis=0, concat_axis=0, tiled=True)  29.6 us
    ppermute x9, waiting for transfers between devices, scatter_sum(): total = total + lax.ppermute(piece, 'feat', moves)  23 us
    unnamed x53, local copies, waits for them, and re-layouts  14.2 us
    gather x6, local copies, waits for them, and re-layouts, pick(): return jnp.take(rows, index, axis=0, mode='clip')  14.1 us
    all_to_all x1, starting transfers between devices, per_device(): lax.all_to_all(key_terms, 'blk', split_axis=0, concat_axis=0, tiled=True)  11.2 us
  transfers between devices with their start and end apart: 18, of which 13 were waited for; matrix products, arithmetic and copies ran while one was open for 13% of the time, Pallas kernels for 0%

profile of v2, /device:TPU:8, one launch (start us, length us, event | category | flops | bytes accessed | tf_op | source)
XLA Modules:
  0.0 293.9 jit_solution(5415080819964581890)
XLA Ops:
  1.0 1.1 select_reduce_fusion.3
  3.1 2.1 gather_fusion
  5.2 17.5 %all-to-all-start = ((bf16[128,2,16,256]{3,2,1,0:T(8,128)(2,1)}), bf16[128,2,16,256]{3,2,1,0:T(8,128)(2,1)S(1)}, u32[]{:S(2)}, u32[]{:S(2)}) async-start(bf16[128,2,16,256]{3,2,1,0:T(8,128)(2,1)} %bitcast.2), calls=%async_computation | async-start | bytes 4194304 | tf_op jit(solution)/shard_map/all_to_all | solution.py:41
  23.0 2.1 gather_fusion.3
  25.1 51.7 %all-to-all-done = bf16[128,2,16,256]{3,2,1,0:T(8,128)(2,1)S(1)} async-done(((bf16[128,2,16,256]{3,2,1,0:T(8,128)(2,1)}), bf16[128,2,16,256]{3,2,1,0:T(8,128)(2,1)S(1)}, u32[]{:S(2)}, u32[]{:S(2)}) %all-to-all-start) | async-done | bytes 2097184 | tf_op jit(solution)/shard_map/all_to_all | solution.py:41
  76.8 1.3 copy-done.9
  78.1 6.1 %all-to-all-start.2 = ((bf16[128,2,16,256]{3,2,1,0:T(8,128)(2,1)}), bf16[128,2,16,256]{3,2,1,0:T(8,128)(2,1)S(1)}, u32[]{:S(2)}, u32[]{:S(2)}) async-start(bf16[128,2,16,256]{3,2,1,0:T(8,128)(2,1)} %bitcast.24), calls=%async_computation.2 | async-start | bytes 4194304 | tf_op jit(solution)/shard_map/all_to_all | solution.py:41
  84.2 1.3 copy.32
  85.6 1.3 copy.30
  86.9 1.6 reshape.404
  88.5 1.7 reshape.396
  90.5 3.2 %gather_fusion.1 = bf16[128,16,256]{2,1,0:T(8,128)(2,1)} fusion(bf16[256,16,256]{2,1,0:T(8,128)(2,1)} %bitcast.125, s32[1024]{0:T(1024)S(1)} %pad_clamp_fusion.4), kind=kCustom, calls=%fused_computation.1 | custom fusion | bytes 2097664 | tf_op jit(solution)/shard_map/jit(_take)/gather | solution.py:36
  93.7 1.6 fusion.33
  95.3 0.9 copy-done.10
  96.3 0.9 dynamic-slice_bitcast_fusion.8
  97.1 3.4 %collective-permute-start = (f32[16,16,256]{2,1,0:T(8,128)}, f32[16,16,256]{2,1,0:T(8,128)S(1)}, u32[]{:S(2)}, u32[]{:S(2)}) collective-permute-start(f32[16,16,256]{2,1,0:T(8,128)} %get-tuple-element.26), channel_id=1, source_target_pairs={{0,1},{1,2},{2,3},{3,0},{4,5},{5,6},{6,7},{7,4},{8,9},{9,10},{10,1... | collective-permute-start | bytes 786440 | tf_op jit(solution)/shard_map/ppermute | solution.py:68
  100.5 3.7 %collective-permute-start.2 = (f32[16,16,256]{2,1,0:T(8,128)}, f32[16,16,256]{2,1,0:T(8,128)}, u32[]{:S(2)}, u32[]{:S(2)}) collective-permute-start(f32[16,16,256]{2,1,0:T(8,128)} %get-tuple-element.27), channel_id=1, source_target_pairs={{0,3},{1,0},{2,1},{3,2},{4,7},{5,4},{6,5},{7,6},{8,11},{9,8},{10,9... | collective-permute-start | bytes 786440 | tf_op jit(solution)/shard_map/ppermute | solution.py:68
  104.2 3.7 %collective-permute-start.1 = (f32[16,16,256]{2,1,0:T(8,128)}, f32[16,16,256]{2,1,0:T(8,128)}, u32[]{:S(2)}, u32[]{:S(2)}) collective-permute-start(f32[16,16,256]{2,1,0:T(8,128)} %get-tuple-element.28), channel_id=1, source_target_pairs={{0,2},{1,3},{2,0},{3,1},{4,6},{5,7},{6,4},{7,5},{8,10},{9,11},{10,... | collective-permute-start | bytes 786440 | tf_op jit(solution)/shard_map/ppermute | solution.py:68
  108.8 6.9 %collective-permute-done.2 = f32[16,16,256]{2,1,0:T(8,128)} collective-permute-done((f32[16,16,256]{2,1,0:T(8,128)}, f32[16,16,256]{2,1,0:T(8,128)}, u32[]{:S(2)}, u32[]{:S(2)}) %collective-permute-start.2) | collective-permute-done | bytes 262176 | tf_op jit(solution)/shard_map/ppermute | solution.py:68
  115.7 1.2 fusion.13
  117.2 2.1 gather_fusion.2
  119.3 19.0 %all-to-all-done.2 = bf16[128,2,16,256]{3,2,1,0:T(8,128)(2,1)S(1)} async-done(((bf16[128,2,16,256]{3,2,1,0:T(8,128)(2,1)}), bf16[128,2,16,256]{3,2,1,0:T(8,128)(2,1)S(1)}, u32[]{:S(2)}, u32[]{:S(2)}) %all-to-all-start.2) | async-done | bytes 2097184 | tf_op jit(solution)/shard_map/all_to_all | solution.py:41
  138.2 1.3 copy-done.8
  139.5 6.1 %all-to-all-start.1 = ((bf16[128,2,16,256]{3,2,1,0:T(8,128)(2,1)}), bf16[128,2,16,256]{3,2,1,0:T(8,128)(2,1)S(1)}, u32[]{:S(2)}, u32[]{:S(2)}) async-start(bf16[128,2,16,256]{3,2,1,0:T(8,128)(2,1)} %bitcast.123), calls=%async_computation.1 | async-start | bytes 4194304 | tf_op jit(solution)/shard_map/all_to_all | solution.py:41
  146.3 0.9 copy.34
  148.8 3.2 %gather_fusion.4 = bf16[128,16,256]{2,1,0:T(8,128)(2,1)} fusion(bf16[256,16,256]{2,1,0:T(8,128)(2,1)} %bitcast.124, s32[1024]{0:T(1024)S(1)} %pad_clamp_fusion.1), kind=kCustom, calls=%fused_computation.4 | custom fusion | bytes 2097664 | tf_op jit(solution)/shard_map/jit(_take)/gather | solution.py:36
  152.0 1.6 fusion.34
  153.6 1.0 copy-done.11
  154.5 0.8 dynamic-slice_bitcast_fusion.5
  155.4 3.4 %collective-permute-start.3 = (f32[16,16,256]{2,1,0:T(8,128)}, f32[16,16,256]{2,1,0:T(8,128)S(1)}, u32[]{:S(2)}, u32[]{:S(2)}) collective-permute-start(f32[16,16,256]{2,1,0:T(8,128)} %get-tuple-element.23), channel_id=1, source_target_pairs={{0,1},{1,2},{2,3},{3,0},{4,5},{5,6},{6,7},{7,4},{8,9},{9,10},{10,1... | collective-permute-start | bytes 786440 | tf_op jit(solution)/shard_map/ppermute | solution.py:68
  158.8 3.7 %collective-permute-start.5 = (f32[16,16,256]{2,1,0:T(8,128)}, f32[16,16,256]{2,1,0:T(8,128)}, u32[]{:S(2)}, u32[]{:S(2)}) collective-permute-start(f32[16,16,256]{2,1,0:T(8,128)} %get-tuple-element.24), channel_id=1, source_target_pairs={{0,3},{1,0},{2,1},{3,2},{4,7},{5,4},{6,5},{7,6},{8,11},{9,8},{10,9... | collective-permute-start | bytes 786440 | tf_op jit(solution)/shard_map/ppermute | solution.py:68
  162.4 3.7 %collective-permute-start.4 = (f32[16,16,256]{2,1,0:T(8,128)S(1)}, f32[16,16,256]{2,1,0:T(8,128)}, u32[]{:S(2)}, u32[]{:S(2)}) collective-permute-start(f32[16,16,256]{2,1,0:T(8,128)S(1)} %get-tuple-element.25), channel_id=1, source_target_pairs={{0,2},{1,3},{2,0},{3,1},{4,6},{5,7},{6,4},{7,5},{8,10},{9,11},{10,... | collective-permute-start | bytes 786440 | tf_op jit(solution)/shard_map/ppermute | solution.py:68
  167.0 6.9 %collective-permute-done.5 = f32[16,16,256]{2,1,0:T(8,128)} collective-permute-done((f32[16,16,256]{2,1,0:T(8,128)}, f32[16,16,256]{2,1,0:T(8,128)}, u32[]{:S(2)}, u32[]{:S(2)}) %collective-permute-start.5) | collective-permute-done | bytes 262176 | tf_op jit(solution)/shard_map/ppermute | solution.py:68
  174.0 1.2 fusion.9
  175.4 5.6 %collective-permute-start.8 = (bf16[16,16,256]{2,1,0:T(8,128)(2,1)S(1)}, bf16[16,16,256]{2,1,0:T(8,128)(2,1)S(1)}, u32[]{:S(2)}, u32[]{:S(2)}) collective-permute-start(bf16[16,16,256]{2,1,0:T(8,128)(2,1)S(1)} %bitcast.135), channel_id=1, source_target_pairs={{0,3},{1,0},{2,1},{3,2},{4,7},{5,4},{6,5},{7,6},{8,11},{9,8},{10,9... | collective-permute-start | bytes 393224 | tf_op jit(solution)/shard_map/ppermute | solution.py:77
  181.0 3.1 %collective-permute-start.7 = (bf16[16,16,256]{2,1,0:T(8,128)(2,1)S(1)}, bf16[16,16,256]{2,1,0:T(8,128)(2,1)S(1)}, u32[]{:S(2)}, u32[]{:S(2)}) collective-permute-start(bf16[16,16,256]{2,1,0:T(8,128)(2,1)S(1)} %bitcast.136), channel_id=1, source_target_pairs={{0,2},{1,3},{2,0},{3,1},{4,6},{5,7},{6,4},{7,5},{8,10},{9,11},{10,... | collective-permute-start | bytes 393224 | tf_op jit(solution)/shard_map/ppermute | solution.py:77
  184.1 2.1 collective-permute-start.6
  186.2 1.2 pad_clamp_fusion
  188.2 2.5 select_n.186.bias_ref
  191.4 0.9 collective-permute-done.6
  192.9 1.0 pad_maximum_fusion
  194.0 1.5 gather_fusion.5
  195.5 1.1 copy.33
  196.6 3.1 %all-to-all-done.1.key_ref = bf16[128,2,16,256]{3,2,1,0:T(8,128)(2,1)S(1)} async-done(((bf16[128,2,16,256]{3,2,1,0:T(8,128)(2,1)}), bf16[128,2,16,256]{3,2,1,0:T(8,128)(2,1)S(1)}, u32[]{:S(2)}, u32[]{:S(2)}) %all-to-all-start.1) | async-done | bytes 2097184 | tf_op jit(solution)/shard_map/all_to_all | solution.py:41
  199.7 1.6 copy-done.1
  201.3 3.1 %score_stats.1 = f32[2,2,512]{2,1,0:T(2,128)S(1)} custom-call(bf16[128,2,16,256]{3,2,1,0:T(8,128)(2,1)S(1)} %all-to-all-done.1.key_ref, bf16[2,512,256]{2,1,0:T(8,128)(2,1)S(1)} %bitcast.115, f32[2,2048,1]{2,1,0:T(8,128)S(1)} %copy-done.1), custom_call_target="tpu_custom_call" | custom-call | tf_op jit(solution)/shard_map/score_stats/pallas_call | solution.py:163
  204.3 3.4 %collective-permute-start.9 = (f32[1,2,2,512]{3,2,1,0:T(2,128)S(1)}, f32[1,2,2,512]{3,2,1,0:T(2,128)S(1)}, u32[]{:S(2)}, u32[]{:S(2)}) collective-permute-start(f32[1,2,2,512]{3,2,1,0:T(2,128)S(1)} %bitcast.119), channel_id=1, source_target_pairs={{0,1},{1,0},{2,3},{3,2},{4,5},{5,4},{6,7},{7,6},{8,9},{9,8},{10,11... | collective-permute-start | bytes 24584 | tf_op jit(solution)/shard_map/ppermute | solution.py:87
  207.8 2.0 collective-permute-done.9
  209.9 4.7 %collective-permute-start.10 = (f32[2,2,2,512]{3,2,1,0:T(2,128)S(1)}, f32[2,2,2,512]{3,2,1,0:T(2,128)S(1)}, u32[]{:S(2)}, u32[]{:S(2)}) collective-permute-start(f32[2,2,2,512]{3,2,1,0:T(2,128)S(1)} %pad_maximum_fusion.2), channel_id=1, source_target_pairs={{0,3},{1,2},{2,1},{3,0},{4,7},{5,6},{6,5},{7,4},{8,11},{9,10},{10,... | collective-permute-start | bytes 49160 | tf_op jit(solution)/shard_map/ppermute | solution.py:87
  214.6 2.1 collective-permute-done.10
  216.8 1.6 copy-done.2
  218.3 5.2 %score_grads.1 = (bf16[128,2,16,256]{3,2,1,0:T(8,128)(2,1)S(1)}, f32[2,512,256]{2,1,0:T(8,128)S(1)}) custom-call(bf16[128,2,16,256]{3,2,1,0:T(8,128)(2,1)S(1)} %all-to-all-done.1.key_ref, bf16[2,512,256]{2,1,0:T(8,128)(2,1)S(1)} %bitcast.116, f32[2,2048,1]{2,1,0:T(8,128)S(1)} %copy-done.2, f32[4,2,2,512]{3,2,1,0:T(2,128)S(1)} %pad_maximum_fusion.1.stats_ref, ...), custom_call_target="tpu_custom_call" | custom-call | tf_op jit(solution)/shard_map/score_grads/pallas_call | solution.py:179
  223.6 1.3 copy-done.3
  224.9 1.0 copy-done.4
  225.8 11.2 %all-to-all-start.3 = ((bf16[128,2,16,256]{3,2,1,0:T(8,128)(2,1)}), bf16[128,2,16,256]{3,2,1,0:T(8,128)(2,1)}, u32[]{:S(2)}, u32[]{:S(2)}) async-start(bf16[128,2,16,256]{3,2,1,0:T(8,128)(2,1)} %copy-done.3), calls=%async_computation.3 | async-start | bytes 4194304 | tf_op jit(solution)/shard_map/all_to_all | solution.py:257
  237.1 2.1 collective-permute-start.11
  239.2 5.0 %collective-permute-start.13 = (f32[16,16,256]{2,1,0:T(8,128)S(1)}, f32[16,16,256]{2,1,0:T(8,128)S(1)}, u32[]{:S(2)}, u32[]{:S(2)}) collective-permute-start(f32[16,16,256]{2,1,0:T(8,128)S(1)} %get-tuple-element.21), channel_id=1, source_target_pairs={{0,3},{1,0},{2,1},{3,2},{4,7},{5,4},{6,5},{7,6},{8,11},{9,8},{10,9... | collective-permute-start | bytes 786440 | tf_op jit(solution)/shard_map/ppermute | solution.py:68
  244.2 2.5 collective-permute-start.12
  246.7 1.9 collective-permute-done.11
  248.6 6.8 %collective-permute-done.13 = f32[16,16,256]{2,1,0:T(8,128)S(1)} collective-permute-done((f32[16,16,256]{2,1,0:T(8,128)S(1)}, f32[16,16,256]{2,1,0:T(8,128)S(1)}, u32[]{:S(2)}, u32[]{:S(2)}) %collective-permute-start.13) | collective-permute-done | bytes 262176 | tf_op jit(solution)/shard_map/ppermute | solution.py:68
  255.4 0.8 fusion.5
  256.2 34.6 %all-to-all-done.3 = bf16[128,2,16,256]{3,2,1,0:T(8,128)(2,1)} async-done(((bf16[128,2,16,256]{3,2,1,0:T(8,128)(2,1)}), bf16[128,2,16,256]{3,2,1,0:T(8,128)(2,1)}, u32[]{:S(2)}, u32[]{:S(2)}) %all-to-all-start.3) | async-done | bytes 2097184 | tf_op jit(solution)/shard_map/all_to_all | solution.py:257
  290.8 2.3 fusion
  293.0 0.9 copy.39
  (93 shorter events, 8.6 us)
Async XLA Ops:
  0.6 93.0 %copy-start = (bf16[16,8,64,16]{2,3,1,0:T(8,128)(2,1)S(1)}, bf16[16,8,64,16]{2,3,1,0:T(8,128)(2,1)}, u32[]{:S(2)}) copy-start(bf16[16,8,64,16]{2,3,1,0:T(8,128)(2,1)} %param.17) | copy-start | bytes 786436
  0.6 2.5 copy-start.6
  5.2 17.8 %copy-start.7 = (bf16[16,16,256]{2,1,0:T(8,128)(2,1)S(1)}, bf16[16,16,256]{2,1,0:T(8,128)(2,1)}, u32[]{:S(2)}) copy-start(bf16[16,16,256]{2,1,0:T(8,128)(2,1)} %param.12) | copy-start | bytes 393220
  5.2 71.6 %all-to-all-start = ((bf16[128,2,16,256]{3,2,1,0:T(8,128)(2,1)}), bf16[128,2,16,256]{3,2,1,0:T(8,128)(2,1)S(1)}, u32[]{:S(2)}, u32[]{:S(2)}) async-start(bf16[128,2,16,256]{3,2,1,0:T(8,128)(2,1)} %bitcast.2), calls=%async_computation | async-start | bytes 4194304 | tf_op jit(solution)/shard_map/all_to_all | solution.py:41
  76.8 1.3 copy-start.9
  76.8 7.4 %copy-start.15 = (s32[2048,8]{0,1:T(8,128)S(1)}, s32[2048,8]{0,1:T(8,128)}, u32[]{:S(2)}) copy-start(s32[2048,8]{0,1:T(8,128)} %param.14) | copy-start | bytes 196612
  76.8 8.8 %copy-start.16 = (s32[2048,8]{0,1:T(8,128)S(1)}, s32[2048,8]{0,1:T(8,128)}, u32[]{:S(2)}) copy-start(s32[2048,8]{0,1:T(8,128)} %param.18) | copy-start | bytes 196612
  78.1 60.1 %all-to-all-start.2 = ((bf16[128,2,16,256]{3,2,1,0:T(8,128)(2,1)}), bf16[128,2,16,256]{3,2,1,0:T(8,128)(2,1)S(1)}, u32[]{:S(2)}, u32[]{:S(2)}) async-start(bf16[128,2,16,256]{3,2,1,0:T(8,128)(2,1)} %bitcast.24), calls=%async_computation.2 | async-start | bytes 4194304 | tf_op jit(solution)/shard_map/all_to_all | solution.py:41
  88.5 5.1 %copy-start.21 = (s32[128,128]{1,0:T(8,128)}, s32[128,128]{1,0:T(8,128)S(1)}, u32[]{:S(2)}) copy-start(s32[128,128]{1,0:T(8,128)S(1)} %reshape.404) | copy-start | bytes 196612
  93.7 14.3 %copy-start.17 = (s32[256,96]{0,1:T(8,128)S(1)}, s32[256,96]{0,1:T(8,128)}, u32[]{:S(2)}) copy-start(s32[256,96]{0,1:T(8,128)} %param.21) | copy-start | bytes 294916
  93.7 14.9 %copy-start.20 = (s32[256,96]{0,1:T(8,128)S(1)}, s32[256,96]{0,1:T(8,128)}, u32[]{:S(2)}) copy-start(s32[256,96]{0,1:T(8,128)} %param.22) | copy-start | bytes 294916
  95.3 1.0 copy-start.10
  95.3 21.7 %copy-start.13 = (bf16[256,256]{1,0:T(8,128)(2,1)S(1)}, bf16[256,256]{1,0:T(8,128)(2,1)}, u32[]{:S(2)}) copy-start(bf16[256,256]{1,0:T(8,128)(2,1)} %param.20) | copy-start | bytes 393220
  97.1 11.7 %collective-permute-start = (f32[16,16,256]{2,1,0:T(8,128)}, f32[16,16,256]{2,1,0:T(8,128)S(1)}, u32[]{:S(2)}, u32[]{:S(2)}) collective-permute-start(f32[16,16,256]{2,1,0:T(8,128)} %get-tuple-element.26), channel_id=1, source_target_pairs={{0,1},{1,2},{2,3},{3,0},{4,5},{5,6},{6,7},{7,4},{8,9},{9,10},{10,1... | collective-permute-start | bytes 786440 | tf_op jit(solution)/shard_map/ppermute | solution.py:68
  100.5 15.2 %collective-permute-start.2 = (f32[16,16,256]{2,1,0:T(8,128)}, f32[16,16,256]{2,1,0:T(8,128)}, u32[]{:S(2)}, u32[]{:S(2)}) collective-permute-start(f32[16,16,256]{2,1,0:T(8,128)} %get-tuple-element.27), channel_id=1, source_target_pairs={{0,3},{1,0},{2,1},{3,2},{4,7},{5,4},{6,5},{7,6},{8,11},{9,8},{10,9... | collective-permute-start | bytes 786440 | tf_op jit(solution)/shard_map/ppermute | solution.py:68
  104.2 11.5 %collective-permute-start.1 = (f32[16,16,256]{2,1,0:T(8,128)}, f32[16,16,256]{2,1,0:T(8,128)}, u32[]{:S(2)}, u32[]{:S(2)}) collective-permute-start(f32[16,16,256]{2,1,0:T(8,128)} %get-tuple-element.28), channel_id=1, source_target_pairs={{0,2},{1,3},{2,0},{3,1},{4,6},{5,7},{6,4},{7,5},{8,10},{9,11},{10,... | collective-permute-start | bytes 786440 | tf_op jit(solution)/shard_map/ppermute | solution.py:68
  138.2 1.3 copy-start.8
  138.2 7.4 %copy-start.18 = (s32[256,96]{0,1:T(8,128)S(1)}, s32[256,96]{0,1:T(8,128)}, u32[]{:S(2)}) copy-start(s32[256,96]{0,1:T(8,128)} %param.21) | copy-start | bytes 294916
  139.5 60.1 %all-to-all-start.1 = ((bf16[128,2,16,256]{3,2,1,0:T(8,128)(2,1)}), bf16[128,2,16,256]{3,2,1,0:T(8,128)(2,1)S(1)}, u32[]{:S(2)}, u32[]{:S(2)}) async-start(bf16[128,2,16,256]{3,2,1,0:T(8,128)(2,1)} %bitcast.123), calls=%async_computation.1 | async-start | bytes 4194304 | tf_op jit(solution)/shard_map/all_to_all | solution.py:41
  145.6 6.3 %copy-start.12 = (bf16[16,8,64,16]{2,3,1,0:T(8,128)(2,1)S(1)}, bf16[16,8,64,16]{2,3,1,0:T(8,128)(2,1)}, u32[]{:S(2)}) copy-start(bf16[16,8,64,16]{2,3,1,0:T(8,128)(2,1)} %param.13) | copy-start | bytes 786436
  147.2 4.8 %copy-start.23 = (s32[2,96]{1,0:T(2,128)}, s32[2,96]{1,0:T(2,128)S(1)}, u32[]{:S(2)}) copy-start(s32[2,96]{1,0:T(2,128)S(1)} %copy.34) | copy-start | bytes 2308
  152.0 14.7 %copy-start.22 = (s32[16,64]{1,0:T(8,128)S(1)}, s32[16,64]{1,0:T(8,128)}, u32[]{:S(2)}) copy-start(s32[16,64]{1,0:T(8,128)} %param.23) | copy-start | bytes 12292
  153.6 1.0 copy-start.11
  155.4 11.7 %collective-permute-start.3 = (f32[16,16,256]{2,1,0:T(8,128)}, f32[16,16,256]{2,1,0:T(8,128)S(1)}, u32[]{:S(2)}, u32[]{:S(2)}) collective-permute-start(f32[16,16,256]{2,1,0:T(8,128)} %get-tuple-element.23), channel_id=1, source_target_pairs={{0,1},{1,2},{2,3},{3,0},{4,5},{5,6},{6,7},{7,4},{8,9},{9,10},{10,1... | collective-permute-start | bytes 786440 | tf_op jit(solution)/shard_map/ppermute | solution.py:68
  158.8 15.2 %collective-permute-start.5 = (f32[16,16,256]{2,1,0:T(8,128)}, f32[16,16,256]{2,1,0:T(8,128)}, u32[]{:S(2)}, u32[]{:S(2)}) collective-permute-start(f32[16,16,256]{2,1,0:T(8,128)} %get-tuple-element.24), channel_id=1, source_target_pairs={{0,3},{1,0},{2,1},{3,2},{4,7},{5,4},{6,5},{7,6},{8,11},{9,8},{10,9... | collective-permute-start | bytes 786440 | tf_op jit(solution)/shard_map/ppermute | solution.py:68
  162.4 11.5 %collective-permute-start.4 = (f32[16,16,256]{2,1,0:T(8,128)S(1)}, f32[16,16,256]{2,1,0:T(8,128)}, u32[]{:S(2)}, u32[]{:S(2)}) collective-permute-start(f32[16,16,256]{2,1,0:T(8,128)S(1)} %get-tuple-element.25), channel_id=1, source_target_pairs={{0,2},{1,3},{2,0},{3,1},{4,6},{5,7},{6,4},{7,5},{8,10},{9,11},{10,... | collective-permute-start | bytes 786440 | tf_op jit(solution)/shard_map/ppermute | solution.py:68
  175.4 16.9 %copy-start.14 = (bf16[256,256]{1,0:T(8,128)(2,1)}, bf16[256,256]{1,0:T(8,128)(2,1)S(1)}, u32[]{:S(2)}) copy-start(bf16[256,256]{1,0:T(8,128)(2,1)S(1)} %fusion.3) | copy-start | bytes 393220
  175.4 16.0 %collective-permute-start.8 = (bf16[16,16,256]{2,1,0:T(8,128)(2,1)S(1)}, bf16[16,16,256]{2,1,0:T(8,128)(2,1)S(1)}, u32[]{:S(2)}, u32[]{:S(2)}) collective-permute-start(bf16[16,16,256]{2,1,0:T(8,128)(2,1)S(1)} %bitcast.135), channel_id=1, source_target_pairs={{0,3},{1,0},{2,1},{3,2},{4,7},{5,4},{6,5},{7,6},{8,11},{9,8},{10,9... | collective-permute-start | bytes 393224 | tf_op jit(solution)/shard_map/ppermute | solution.py:77
  181.0 10.4 %collective-permute-start.7 = (bf16[16,16,256]{2,1,0:T(8,128)(2,1)S(1)}, bf16[16,16,256]{2,1,0:T(8,128)(2,1)S(1)}, u32[]{:S(2)}, u32[]{:S(2)}) collective-permute-start(bf16[16,16,256]{2,1,0:T(8,128)(2,1)S(1)} %bitcast.136), channel_id=1, source_target_pairs={{0,2},{1,3},{2,0},{3,1},{4,6},{5,7},{6,4},{7,5},{8,10},{9,11},{10,... | collective-permute-start | bytes 393224 | tf_op jit(solution)/shard_map/ppermute | solution.py:77
  184.1 8.2 %collective-permute-start.6 = (bf16[16,16,256]{2,1,0:T(8,128)(2,1)S(1)}, bf16[16,16,256]{2,1,0:T(8,128)(2,1)S(1)}, u32[]{:S(2)}, u32[]{:S(2)}) collective-permute-start(bf16[16,16,256]{2,1,0:T(8,128)(2,1)S(1)} %bitcast.137), channel_id=1, source_target_pairs={{0,1},{1,2},{2,3},{3,0},{4,5},{5,6},{6,7},{7,4},{8,9},{9,10},{10,1... | collective-permute-start | bytes 393224 | tf_op jit(solution)/shard_map/ppermute | solution.py:77
  192.3 0.7 copy-start.19
  199.7 1.6 copy-start.1
  204.3 5.5 %collective-permute-start.9 = (f32[1,2,2,512]{3,2,1,0:T(2,128)S(1)}, f32[1,2,2,512]{3,2,1,0:T(2,128)S(1)}, u32[]{:S(2)}, u32[]{:S(2)}) collective-permute-start(f32[1,2,2,512]{3,2,1,0:T(2,128)S(1)} %bitcast.119), channel_id=1, source_target_pairs={{0,1},{1,0},{2,3},{3,2},{4,5},{5,4},{6,7},{7,6},{8,9},{9,8},{10,11... | collective-permute-start | bytes 24584 | tf_op jit(solution)/shard_map/ppermute | solution.py:87
  209.9 6.8 %collective-permute-start.10 = (f32[2,2,2,512]{3,2,1,0:T(2,128)S(1)}, f32[2,2,2,512]{3,2,1,0:T(2,128)S(1)}, u32[]{:S(2)}, u32[]{:S(2)}) collective-permute-start(f32[2,2,2,512]{3,2,1,0:T(2,128)S(1)} %pad_maximum_fusion.2), channel_id=1, source_target_pairs={{0,3},{1,2},{2,1},{3,0},{4,7},{5,6},{6,5},{7,4},{8,11},{9,10},{10,... | collective-permute-start | bytes 49160 | tf_op jit(solution)/shard_map/ppermute | solution.py:87
  216.7 1.6 copy-start.2
  223.5 1.3 copy-start.3
  224.9 1.0 copy-start.4
  225.8 11.2 %copy-start.5 = (f32[2,512,256]{2,1,0:T(8,128)S(1)}, f32[2,512,256]{2,1,0:T(8,128)}, u32[]{:S(2)}) copy-start(f32[2,512,256]{2,1,0:T(8,128)} %copy-done.4) | copy-start | bytes 3145732
  225.8 64.9 %all-to-all-start.3 = ((bf16[128,2,16,256]{3,2,1,0:T(8,128)(2,1)}), bf16[128,2,16,256]{3,2,1,0:T(8,128)(2,1)}, u32[]{:S(2)}, u32[]{:S(2)}) async-start(bf16[128,2,16,256]{3,2,1,0:T(8,128)(2,1)} %copy-done.3), calls=%async_computation.3 | async-start | bytes 4194304 | tf_op jit(solution)/shard_map/all_to_all | solution.py:257
  237.0 53.7 %copy-start.24 = (pred[256]{0:T(512)(128)(4,1)S(1)}, pred[256]{0:T(512)(128)(4,1)}, u32[]{:S(2)}) copy-start(pred[256]{0:T(512)(128)(4,1)} %get-tuple-element.18) | copy-start | bytes 772
  237.1 11.5 %collective-permute-start.11 = (f32[16,16,256]{2,1,0:T(8,128)S(1)}, f32[16,16,256]{2,1,0:T(8,128)S(1)}, u32[]{:S(2)}, u32[]{:S(2)}) collective-permute-start(f32[16,16,256]{2,1,0:T(8,128)S(1)} %get-tuple-element.20), channel_id=1, source_target_pairs={{0,1},{1,2},{2,3},{3,0},{4,5},{5,6},{6,7},{7,4},{8,9},{9,10},{10,1... | collective-permute-start | bytes 786440 | tf_op jit(solution)/shard_map/ppermute | solution.py:68
  239.2 16.2 %collective-permute-start.13 = (f32[16,16,256]{2,1,0:T(8,128)S(1)}, f32[16,16,256]{2,1,0:T(8,128)S(1)}, u32[]{:S(2)}, u32[]{:S(2)}) collective-permute-start(f32[16,16,256]{2,1,0:T(8,128)S(1)} %get-tuple-element.21), channel_id=1, source_target_pairs={{0,3},{1,0},{2,1},{3,2},{4,7},{5,4},{6,5},{7,6},{8,11},{9,8},{10,9... | collective-permute-start | bytes 786440 | tf_op jit(solution)/shard_map/ppermute | solution.py:68
  244.2 11.2 %collective-permute-start.12 = (f32[16,16,256]{2,1,0:T(8,128)S(1)}, f32[16,16,256]{2,1,0:T(8,128)S(1)}, u32[]{:S(2)}, u32[]{:S(2)}) collective-permute-start(f32[16,16,256]{2,1,0:T(8,128)S(1)} %get-tuple-element.22), channel_id=1, source_target_pairs={{0,2},{1,3},{2,0},{3,1},{4,6},{5,7},{6,4},{7,5},{8,10},{9,11},{10,... | collective-permute-start | bytes 786440 | tf_op jit(solution)/shard_map/ppermute | solution.py:68
